TPU v7x, 32 devices: a whole 2x2x4 slice. The times are simulated.
32 devices in a mesh: dp: 8 (over z, x), tensor: 4 (over y, core).
Axes of the slice: x: 2, y: 2, z: 4, core: 2. Of those that a mesh axis runs over, the one named last changes fastest.
Arguments:
- hidden_in: bfloat16 [16384, 640], P('dp'), may hold values from -6 to 6
- query_weight: bfloat16 [640, 1024], P(None, 'tensor'), may hold values from -0.25 to 0.25
- key_weight: bfloat16 [640, 256], replicated, may hold values from -0.25 to 0.25
- value_weight: bfloat16 [640, 256], replicated, may hold values from -0.25 to 0.25
- output_weight: bfloat16 [1024, 640], P('tensor'), may hold values from -0.1875 to 0.1875
- gate_weight: bfloat16 [640, 2048], P(None, 'tensor'), may hold values from -0.25 to 0.25
- up_weight: bfloat16 [640, 2048], P(None, 'tensor'), may hold values from -0.25 to 0.25
- down_weight: bfloat16 [2048, 640], P('tensor'), may hold values from -0.125 to 0.125
- pre_attention: float32 [640], replicated, may hold values from -0.5 to 0.5
- query_norm: float32 [256], replicated, may hold values from -0.5 to 0.5
- key_norm: float32 [256], replicated, may hold values from -0.5 to 0.5
- post_attention: float32 [640], replicated, may hold values from -0.5 to 0.5
- pre_feedforward: float32 [640], replicated, may hold values from -0.5 to 0.5
- post_feedforward: float32 [640], replicated, may hold values from -0.5 to 0.5
- segments: int32 [16384], P('dp'), may hold values from 0 to 15, as said below
- positions: int32 [16384], P('dp'), may hold values from 0 to 511, as said below
- cotangent: bfloat16 [16384, 640], P('dp'), may hold values from -6 to 6
Outputs:
- hidden_out: bfloat16 [16384, 640], P('dp')
- grad_input: float32 [16384, 640], P('dp')
- grad_query_weight: float32 [640, 1024], P(None, 'tensor')
- grad_key_weight: float32 [640, 256], replicated
- grad_value_weight: float32 [640, 256], replicated
- grad_output_weight: float32 [1024, 640], P('tensor')
- grad_gate_weight: float32 [640, 2048], P(None, 'tensor')
- grad_up_weight: float32 [640, 2048], P(None, 'tensor')
- grad_down_weight: float32 [2048, 640], P('tensor')
- grad_pre_attention: float32 [640], replicated
- grad_query_norm: float32 [256], replicated
- grad_key_norm: float32 [256], replicated
- grad_post_attention: float32 [640], replicated
- grad_pre_feedforward: float32 [640], replicated
- grad_post_feedforward: float32 [640], replicated
Inputs may be any that keep to these rules, and one draw needn't show every extreme that they name: `segments`: within each aligned block of 512 tokens the document numbers start at 0 at the block's first token and rise by 0 or 1 from one token to the next. `positions`: each token's position is its distance from the first token of its document in the same block.
All inputs are finite; a program needn't handle non-finite values.
Results may differ from a plain program's by a relative error of at most 0.02.
Values may be sent and summed in bfloat16 or wider, within the bound.
A program may use at most 128 MiB of HBM per device.

v0:
```python
import jax
import jax.numpy as jnp
from jax import lax
from jax.sharding import PartitionSpec as P

LEN = 512
epsilon = 1e-06
rope_base = 1000000.0
masked_score = -1e30


def normed(values, norm_gain):
    inverse = lax.rsqrt(jnp.mean(values * values, axis=-1, keepdims=True) + epsilon)
    return values * inverse * (1.0 + norm_gain)


def rotary(values, cosine, sine_table):
    half_width = values.shape[-1] // 2
    front_half = values[..., :half_width]
    second = values[..., half_width:]
    return jnp.concatenate(
        [front_half * cosine - second * sine_table, second * cosine + front_half * sine_table],
        axis=-1,
    )


def rotary_tables(positions, head_width):
    steps_half = jnp.arange(head_width // 2).astype(jnp.float32)
    frequency = jnp.power(jnp.float32(rope_base), -2.0 * steps_half / head_width)
    angles = positions.astype(jnp.float32)[:, None] * frequency[None, :]
    return (jnp.cos(angles), jnp.sin(angles))


def gated(gate_proj, up_proj):
    return jax.nn.gelu(gate_proj, approximate=True) * up_proj


def pack_mask(segment):
    offsets = jnp.arange(segment.shape[0])
    return (segment[:, None] == segment[None, :]) & (offsets[None, :] <= offsets[:, None])


def pack_scores(queries, key_rows, segment):
    score_scale = queries.shape[-1] ** (-0.5)
    scores = (
        jnp.einsum("ihd,jd->hij", queries, key_rows, preferred_element_type=jnp.float32)
        * score_scale
    )
    return jnp.where(pack_mask(segment)[None], scores, masked_score)


def attend_pack(inputs):
    queries, key_rows, values, segment = inputs
    scores = pack_scores(queries, key_rows, segment)
    top_score = jnp.max(scores, axis=-1, keepdims=True)
    log_total = top_score + jnp.log(jnp.sum(jnp.exp(scores - top_score), axis=-1, keepdims=True))
    prob_low = jnp.exp(scores - log_total).astype(jnp.bfloat16)
    mixture = jnp.einsum("hij,jd->ihd", prob_low, values, preferred_element_type=jnp.float32)
    return (mixture.astype(jnp.bfloat16), log_total)


def attend_back(inputs):
    queries, key_rows, values, segment, log_total, mixture_grad = inputs
    score_scale = queries.shape[-1] ** (-0.5)
    probability = jnp.exp(pack_scores(queries, key_rows, segment) - log_total)
    prob_low = probability.astype(jnp.bfloat16)
    value_grad = jnp.einsum(
        "hij,ihd->jhd", prob_low, mixture_grad, preferred_element_type=jnp.float32
    )
    prob_grad = jnp.einsum("ihd,jd->hij", mixture_grad, values, preferred_element_type=jnp.float32)
    row_terms = jnp.sum(probability * prob_grad, axis=-1, keepdims=True)
    score_grad = (probability * (prob_grad - row_terms)).astype(jnp.bfloat16)
    query_grad = (
        jnp.einsum("hij,jd->ihd", score_grad, key_rows, preferred_element_type=jnp.float32)
        * score_scale
    )
    key_grad = (
        jnp.einsum("hij,ihd->jhd", score_grad, queries, preferred_element_type=jnp.float32)
        * score_scale
    )
    return (query_grad, key_grad, value_grad.astype(jnp.bfloat16))


def run_layer(
    hidden_in,
    query_weight,
    key_weight,
    value_weight,
    output_weight,
    gate_weight,
    up_weight,
    down_weight,
    pre_attention,
    query_norm,
    key_norm,
    post_attention,
    pre_feedforward,
    post_feedforward,
    segments,
    positions,
    cotangent,
    reducers,
    feed_hook,
):
    attention_reduce, feed_reduce, feed_back_reduce, attention_back_reduce = reducers
    tokens = hidden_in.shape[0]
    pack_length = LEN
    pack_count = tokens // pack_length
    head_width = key_weight.shape[1]
    local_heads = query_weight.shape[1] // head_width
    hidden = hidden_in.astype(jnp.float32)
    cosine, sine_table = rotary_tables(positions, head_width)

    def head_path(projected, norm_gain):
        return rotary(normed(projected, norm_gain), cosine[:, None, :], sine_table[:, None, :])

    normed_value, pre_back = jax.vjp(normed, hidden, pre_attention)
    normed_in = normed_value.astype(jnp.bfloat16)
    query_proj = jnp.dot(normed_in, query_weight, preferred_element_type=jnp.float32)
    query_proj = query_proj.reshape(tokens, local_heads, head_width)
    key_proj = jnp.dot(normed_in, key_weight, preferred_element_type=jnp.float32)
    value_low = jnp.dot(normed_in, value_weight, preferred_element_type=jnp.float32).astype(
        jnp.bfloat16
    )
    query_rot, query_back = jax.vjp(head_path, query_proj, query_norm)
    key_heads = key_proj[:, None, :]
    key_rot, key_back = jax.vjp(head_path, key_heads, key_norm)
    query_packs = query_rot.astype(jnp.bfloat16).reshape(
        pack_count, pack_length, local_heads, head_width
    )
    key_packs = key_rot[:, 0, :].astype(jnp.bfloat16).reshape(pack_count, pack_length, head_width)
    value_packs = value_low.reshape(pack_count, pack_length, head_width)
    segment_packs = segments.reshape(pack_count, pack_length)
    mixture, log_total = lax.map(attend_pack, (query_packs, key_packs, value_packs, segment_packs))
    mixture_low = mixture.reshape(tokens, local_heads * head_width)
    attention = attention_reduce(
        jnp.dot(mixture_low, output_weight, preferred_element_type=jnp.float32)
    )
    post_value, post_att_back = jax.vjp(normed, attention, post_attention)
    middle = hidden + post_value
    mid_value, mid_back = jax.vjp(normed, middle, pre_feedforward)
    normed_mid = mid_value.astype(jnp.bfloat16)
    gate_proj = jnp.dot(normed_mid, gate_weight, preferred_element_type=jnp.float32)
    up_proj = jnp.dot(normed_mid, up_weight, preferred_element_type=jnp.float32)
    product, gated_back = jax.vjp(gated, gate_proj, up_proj)
    product_low = product.astype(jnp.bfloat16)
    feed = feed_reduce(jnp.dot(product_low, down_weight, preferred_element_type=jnp.float32))
    feed_value, feed_out_back = jax.vjp(normed, feed, post_feedforward)
    hidden_out = (middle + feed_value).astype(jnp.bfloat16)
    cotangent_full = cotangent.astype(jnp.float32)
    feed_grad, grad_post_feedforward = feed_out_back(cotangent_full)
    feed_grad_low = feed_grad.astype(jnp.bfloat16)
    grad_down_weight = jnp.einsum(
        "tf,td->fd", product_low, feed_grad_low, preferred_element_type=jnp.float32
    )
    product_grad = jnp.einsum(
        "td,fd->tf", feed_grad_low, down_weight, preferred_element_type=jnp.float32
    )
    gate_grad, up_grad = gated_back(product_grad)
    gate_grad_low = gate_grad.astype(jnp.bfloat16)
    up_grad_low = up_grad.astype(jnp.bfloat16)
    grad_gate_weight = jnp.einsum(
        "td,tf->df", normed_mid, gate_grad_low, preferred_element_type=jnp.float32
    )
    grad_up_weight = jnp.einsum(
        "td,tf->df", normed_mid, up_grad_low, preferred_element_type=jnp.float32
    )
    grad_gate_weight, grad_up_weight, grad_down_weight, grad_post_feedforward = feed_hook(
        (grad_gate_weight, grad_up_weight, grad_down_weight, grad_post_feedforward)
    )
    mid_part = jnp.einsum(
        "tf,df->td", gate_grad_low, gate_weight, preferred_element_type=jnp.float32
    )
    mid_part = mid_part + jnp.einsum(
        "tf,df->td", up_grad_low, up_weight, preferred_element_type=jnp.float32
    )
    mid_normed_grad = feed_back_reduce(mid_part)
    middle_part, grad_pre_feedforward = mid_back(mid_normed_grad)
    middle_grad = cotangent_full + middle_part
    attention_grad, grad_post_attention = post_att_back(middle_grad)
    attention_grad_low = attention_grad.astype(jnp.bfloat16)
    grad_output_weight = jnp.einsum(
        "tk,td->kd", mixture_low, attention_grad_low, preferred_element_type=jnp.float32
    )
    mixture_grad = jnp.einsum(
        "td,kd->tk", attention_grad_low, output_weight, preferred_element_type=jnp.float32
    )
    mixture_grad_packs = mixture_grad.astype(jnp.bfloat16).reshape(
        pack_count, pack_length, local_heads, head_width
    )
    query_rot_grad, key_rot_grad, value_grad_low = lax.map(
        attend_back,
        (query_packs, key_packs, value_packs, segment_packs, log_total, mixture_grad_packs),
    )
    query_grad, grad_query_norm = query_back(
        query_rot_grad.reshape(tokens, local_heads, head_width)
    )
    key_grad, grad_key_norm = key_back(key_rot_grad.reshape(tokens, local_heads, head_width))
    query_grad_low = query_grad.astype(jnp.bfloat16).reshape(tokens, local_heads * head_width)
    key_grad_low = key_grad.astype(jnp.bfloat16)
    value_grad_low = value_grad_low.reshape(tokens, local_heads, head_width)
    grad_query_weight = jnp.einsum(
        "td,tk->dk", normed_in, query_grad_low, preferred_element_type=jnp.float32
    )
    grad_key_weight = jnp.einsum(
        "td,thk->dk", normed_in, key_grad_low, preferred_element_type=jnp.float32
    )
    grad_value_weight = jnp.einsum(
        "td,thk->dk", normed_in, value_grad_low, preferred_element_type=jnp.float32
    )
    in_part = jnp.einsum(
        "tk,dk->td", query_grad_low, query_weight, preferred_element_type=jnp.float32
    )
    in_part = in_part + jnp.einsum(
        "thk,dk->td", key_grad_low, key_weight, preferred_element_type=jnp.float32
    )
    in_part = in_part + jnp.einsum(
        "thk,dk->td", value_grad_low, value_weight, preferred_element_type=jnp.float32
    )
    in_normed_grad = attention_back_reduce(in_part)
    input_part, grad_pre_attention = pre_back(in_normed_grad)
    grad_input = middle_grad + input_part
    return (
        hidden_out,
        grad_input,
        grad_query_weight,
        grad_key_weight,
        grad_value_weight,
        grad_output_weight,
        grad_gate_weight,
        grad_up_weight,
        grad_down_weight,
        grad_pre_attention,
        grad_query_norm,
        grad_key_norm,
        grad_post_attention,
        grad_pre_feedforward,
        grad_post_feedforward,
    )


def on_device(
    hidden_in,
    query_weight,
    key_weight,
    value_weight,
    output_weight,
    gate_weight,
    up_weight,
    down_weight,
    pre_attention,
    query_norm,
    key_norm,
    post_attention,
    pre_feedforward,
    post_feedforward,
    segments,
    positions,
    cotangent,
):

    def attention_reduce(values):
        return lax.psum(values, "tensor")

    def feed_reduce(values):
        return lax.psum(values.astype(jnp.bfloat16), "tensor").astype(jnp.float32)

    def feed_back_reduce(values):
        return lax.psum(values.astype(jnp.bfloat16), "tensor").astype(jnp.float32)

    def attention_back_reduce(values):
        return lax.psum(values.astype(jnp.bfloat16), "tensor").astype(jnp.float32)

    def feed_hook(grads):
        return grads

    (
        hidden_out,
        grad_input,
        grad_query_weight,
        grad_key_weight,
        grad_value_weight,
        grad_output_weight,
        grad_gate_weight,
        grad_up_weight,
        grad_down_weight,
        grad_pre_attention,
        grad_query_norm,
        grad_key_norm,
        grad_post_attention,
        grad_pre_feedforward,
        grad_post_feedforward,
    ) = run_layer(
        hidden_in,
        query_weight,
        key_weight,
        value_weight,
        output_weight,
        gate_weight,
        up_weight,
        down_weight,
        pre_attention,
        query_norm,
        key_norm,
        post_attention,
        pre_feedforward,
        post_feedforward,
        segments,
        positions,
        cotangent,
        (attention_reduce, feed_reduce, feed_back_reduce, attention_back_reduce),
        feed_hook,
    )
    grad_key_weight, grad_value_weight, grad_query_norm, grad_key_norm = lax.psum(
        (grad_key_weight, grad_value_weight, grad_query_norm, grad_key_norm), ("dp", "tensor")
    )
    (
        grad_query_weight,
        grad_output_weight,
        grad_gate_weight,
        grad_up_weight,
        grad_down_weight,
        grad_pre_attention,
        grad_post_attention,
        grad_pre_feedforward,
        grad_post_feedforward,
    ) = lax.psum(
        (
            grad_query_weight,
            grad_output_weight,
            grad_gate_weight,
            grad_up_weight,
            grad_down_weight,
            grad_pre_attention,
            grad_post_attention,
            grad_pre_feedforward,
            grad_post_feedforward,
        ),
        "dp",
    )
    return (
        hidden_out,
        grad_input,
        grad_query_weight,
        grad_key_weight,
        grad_value_weight,
        grad_output_weight,
        grad_gate_weight,
        grad_up_weight,
        grad_down_weight,
        grad_pre_attention,
        grad_query_norm,
        grad_key_norm,
        grad_post_attention,
        grad_pre_feedforward,
        grad_post_feedforward,
    )


def solution(mesh):
    placed = (
        P("dp", None),
        P(None, "tensor"),
        P(),
        P(),
        P("tensor", None),
        P(None, "tensor"),
        P(None, "tensor"),
        P("tensor", None),
        P(),
        P(),
        P(),
        P(),
        P(),
        P(),
        P("dp"),
        P("dp"),
        P("dp", None),
    )
    return jax.shard_map(
        on_device,
        mesh=mesh,
        in_specs=placed,
        out_specs=(
            P("dp", None),
            P("dp", None),
            P(None, "tensor"),
            P(),
            P(),
            P("tensor", None),
            P(None, "tensor"),
            P(None, "tensor"),
            P("tensor", None),
            P(),
            P(),
            P(),
            P(),
            P(),
            P(),
        ),
        check_vma=False,
    )
```

profile of v0, /device:TPU:0, one launch (start us, length us, event | category | flops | bytes accessed | tf_op | source)
XLA Modules:
  0.0 909.8 jit_solution(12823472843531258651)
XLA Ops:
  7.3 2.5 fusion.63
  10.8 2.4 multiply_reduce_fusion.6
  13.2 2.3 multiply_reduce_fusion.5
  15.6 3.0 copy.42
  18.6 2.6 multiply_bitcast_fusion
  21.3 5.7 fusion.99
  31.1 2.3 pad_maximum_fusion
  33.4 2.3 copy.56
  35.6 3.7 convolution_convert_fusion.4
  40.0 2.3 pad_maximum_fusion.1
  43.3 26.9 %while.26 = (s32[]{:T(128)}, bf16[4,512,1,256]{3,1,0,2:T(8,128)(2,1)}, f32[4,1,512,1]{2,3,1,0:T(1,128)}, bf16[4,512,256]{2,1,0:T(8,128)(2,1)}, s32[4,512]{1,0:T(...) while((s32[]{:T(128)}, bf16[4,512,1,256]{3,1,0,2:T(8,128)(2,1)}, ...), condition=%wide.region_6.7_spmd, body=%wide.region_3.6_spmd.sunk | while | flops 271187456 | bytes 5272153 | solution.py:134
  70.2 4.6 fusion.115
  75.6 104.7 %all-reduce.15.cloned.1.call-done = f32[2048,640]{1,0:T(8,128)} async-done(((f32[2048,640]{1,0:T(8,128)}), f32[2048,640]{1,0:T(8,128)}) %all-reduce.15.cloned.1.call-update) | async-done | bytes 5242896 | tf_op jit(solution)/shard_map/psum | solution.py:263
  180.3 3.0 multiply_reduce_fusion.4
  190.1 4.1 multiply_convert_fusion.3
  195.5 3.3 convolution_convert_fusion.2
  199.4 59.6 %all-reduce.17.cloned.1.call-done = bf16[2048,640]{1,0:T(8,128)(2,1)} async-done(((bf16[2048,640]{1,0:T(8,128)(2,1)}), bf16[2048,640]{1,0:T(8,128)(2,1)}) %all-reduce.17.cloned.1.call-update) | async-done | bytes 2621456 | tf_op jit(solution)/shard_map/psum | solution.py:266
  259.0 2.5 fusion.61
  261.5 4.2 fusion.57
  267.9 4.9 multiply_convert_fusion.2
  274.8 3.3 add_convert_fusion.1
  278.4 5.3 fusion.126
  283.6 54.6 %all-reduce.19.cloned.1.call-done = bf16[2048,640]{1,0:T(8,128)(2,1)} async-done(((bf16[2048,640]{1,0:T(8,128)(2,1)}), bf16[2048,640]{1,0:T(8,128)(2,1)}) %all-reduce.19.cloned.1.call-update) | async-done | bytes 2621456 | tf_op jit(solution)/shard_map/psum | solution.py:269
  338.3 4.4 fusion.55
  343.1 7.7 multiply_reduce_fusion.1
  355.8 125.7 %while.27 = (s32[]{:T(128)}, f32[4,512,1,256]{1,0,3,2:T(4,128)}, f32[4,512,1,256]{1,0,3,2:T(4,128)}, bf16[4,512,1,256]{3,1,0,2:T(8,128)(2,1)}, bf16[4,512,256]{2...) while((s32[]{:T(128)}, f32[4,512,1,256]{1,0,3,2:T(4,128)}, ...), condition=%wide.region_18.19_spmd, body=%wide.region_16.18_spmd.sunk | while | flops 674627072 | bytes 16275081 | solution.py:191
  362.1 11.0 %dynamic_update_slice.30 = f32[4,512,1,256]{1,0,3,2:T(4,128)} dynamic-update-slice(f32[4,512,1,256]{1,0,3,2:T(4,128)} %get-tuple-element.387, f32[1,512,1,256]{1,0,3,2:T(1,128)S(1)} %copy.93, s32[]{:T(128)} %get-tuple-element.385, s32[]{:T(128)} %constant.83.clone.1..sunk, s32[]{:T(128)} %constant.83.clone.1..sunk, s32[]{:T(128)} %constant.83.clone.1..sunk) | dynamic-update-slice | bytes 1048580 | tf_op jit(solution)/shard_map/while/body/jit(dynamic_update_index_in_dim)/dynamic_update_slice | solution.py:191
  374.9 11.1 %dynamic_update_slice.29 = f32[4,512,1,256]{1,0,3,2:T(4,128)} dynamic-update-slice(f32[4,512,1,256]{1,0,3,2:T(4,128)} %get-tuple-element.386, f32[1,512,1,256]{1,0,3,2:T(1,128)S(1)} %copy.92, s32[]{:T(128)} %get-tuple-element.385, s32[]{:T(128)} %constant.83.clone.1..sunk, s32[]{:T(128)} %constant.83.clone.1..sunk, s32[]{:T(128)} %constant.83.clone.1..sunk) | dynamic-update-slice | bytes 1048580 | tf_op jit(solution)/shard_map/while/body/jit(dynamic_update_index_in_dim)/dynamic_update_slice | solution.py:191
  393.5 11.0 %dynamic_update_slice.30 = f32[4,512,1,256]{1,0,3,2:T(4,128)} dynamic-update-slice(f32[4,512,1,256]{1,0,3,2:T(4,128)} %get-tuple-element.387, f32[1,512,1,256]{1,0,3,2:T(1,128)S(1)} %copy.93, s32[]{:T(128)} %get-tuple-element.385, s32[]{:T(128)} %constant.83.clone.1..sunk, s32[]{:T(128)} %constant.83.clone.1..sunk, s32[]{:T(128)} %constant.83.clone.1..sunk) | dynamic-update-slice | bytes 1048580 | tf_op jit(solution)/shard_map/while/body/jit(dynamic_update_index_in_dim)/dynamic_update_slice | solution.py:191
  406.3 11.1 %dynamic_update_slice.29 = f32[4,512,1,256]{1,0,3,2:T(4,128)} dynamic-update-slice(f32[4,512,1,256]{1,0,3,2:T(4,128)} %get-tuple-element.386, f32[1,512,1,256]{1,0,3,2:T(1,128)S(1)} %copy.92, s32[]{:T(128)} %get-tuple-element.385, s32[]{:T(128)} %constant.83.clone.1..sunk, s32[]{:T(128)} %constant.83.clone.1..sunk, s32[]{:T(128)} %constant.83.clone.1..sunk) | dynamic-update-slice | bytes 1048580 | tf_op jit(solution)/shard_map/while/body/jit(dynamic_update_index_in_dim)/dynamic_update_slice | solution.py:191
  425.0 11.0 %dynamic_update_slice.30 = f32[4,512,1,256]{1,0,3,2:T(4,128)} dynamic-update-slice(f32[4,512,1,256]{1,0,3,2:T(4,128)} %get-tuple-element.387, f32[1,512,1,256]{1,0,3,2:T(1,128)S(1)} %copy.93, s32[]{:T(128)} %get-tuple-element.385, s32[]{:T(128)} %constant.83.clone.1..sunk, s32[]{:T(128)} %constant.83.clone.1..sunk, s32[]{:T(128)} %constant.83.clone.1..sunk) | dynamic-update-slice | bytes 1048580 | tf_op jit(solution)/shard_map/while/body/jit(dynamic_update_index_in_dim)/dynamic_update_slice | solution.py:191
  437.8 11.1 %dynamic_update_slice.29 = f32[4,512,1,256]{1,0,3,2:T(4,128)} dynamic-update-slice(f32[4,512,1,256]{1,0,3,2:T(4,128)} %get-tuple-element.386, f32[1,512,1,256]{1,0,3,2:T(1,128)S(1)} %copy.92, s32[]{:T(128)} %get-tuple-element.385, s32[]{:T(128)} %constant.83.clone.1..sunk, s32[]{:T(128)} %constant.83.clone.1..sunk, s32[]{:T(128)} %constant.83.clone.1..sunk) | dynamic-update-slice | bytes 1048580 | tf_op jit(solution)/shard_map/while/body/jit(dynamic_update_index_in_dim)/dynamic_update_slice | solution.py:191
  456.4 11.0 %dynamic_update_slice.30 = f32[4,512,1,256]{1,0,3,2:T(4,128)} dynamic-update-slice(f32[4,512,1,256]{1,0,3,2:T(4,128)} %get-tuple-element.387, f32[1,512,1,256]{1,0,3,2:T(1,128)S(1)} %copy.93, s32[]{:T(128)} %get-tuple-element.385, s32[]{:T(128)} %constant.83.clone.1..sunk, s32[]{:T(128)} %constant.83.clone.1..sunk, s32[]{:T(128)} %constant.83.clone.1..sunk) | dynamic-update-slice | bytes 1048580 | tf_op jit(solution)/shard_map/while/body/jit(dynamic_update_index_in_dim)/dynamic_update_slice | solution.py:191
  469.2 11.1 %dynamic_update_slice.29 = f32[4,512,1,256]{1,0,3,2:T(4,128)} dynamic-update-slice(f32[4,512,1,256]{1,0,3,2:T(4,128)} %get-tuple-element.386, f32[1,512,1,256]{1,0,3,2:T(1,128)S(1)} %copy.92, s32[]{:T(128)} %get-tuple-element.385, s32[]{:T(128)} %constant.83.clone.1..sunk, s32[]{:T(128)} %constant.83.clone.1..sunk, s32[]{:T(128)} %constant.83.clone.1..sunk) | dynamic-update-slice | bytes 1048580 | tf_op jit(solution)/shard_map/while/body/jit(dynamic_update_index_in_dim)/dynamic_update_slice | solution.py:191
  481.5 2.7 reshape.588
  484.2 3.7 reshape.591
  487.9 7.3 fusion.104
  502.2 2.5 add_convert_fusion
  506.5 4.3 fusion.124
  510.8 2.6 fusion.125
  517.0 4.1 fusion.123
  522.9 40.3 %all-reduce.4 = (f32[256]{0:T(256)}, f32[256]{0:T(256)}) all-reduce(f32[256]{0:T(256)S(1)} %get-tuple-element.156, f32[256]{0:T(256)S(1)} %get-tuple-element.154), channel_id=1, replica_groups=mesh['dp'=8,'tensor'=4] {'dp','tensor'}, use_global_device_ids=true, to_apply=%region_33.34 | all-reduce | flops 512 | bytes 4096 | tf_op jit(solution)/shard_map/psum | solution.py:314
  563.1 3.0 all-reduce.21.cloned.1.call-done
  566.2 4.0 fusion.56
  570.2 37.7 %all-reduce.6 = (f32[640]{0:T(1024)}, f32[640]{0:T(1024)}, f32[640]{0:T(1024)}, f32[640]{0:T(1024)}) all-reduce(f32[640]{0:T(1024)S(1)} %get-tuple-element.152, f32[640]{0:T(1024)S(1)} %get-tuple-element.146, f32[640]{0:T(1024)S(1)} %get-tuple-element.148, f32[640]{0:T(1024)S(1)} %get-tuple-element.150), channel_id=1, replica_groups=mesh['dp'=8,'tensor'=4] {'dp'}, use_global_device_ids=true, to_apply=%region_31.32 | all-reduce | flops 2560 | bytes 20480 | tf_op jit(solution)/shard_map/psum | solution.py:327
  607.9 5.5 fusion.60
  613.4 90.6 %all-reduce.23.cloned.1.call-done = (f32[640,256]{1,0:T(8,128)}, f32[640,256]{1,0:T(8,128)}) async-done(((f32[640,256]{1,0:T(8,128)}, f32[640,256]{1,0:T(8,128)}), (f32[640,256]{1,0:T(8,128)}, f32[640,256]{1,0:T(8,128)})) %all-reduce.23.cloned.1.call-update) | async-done | bytes 1310736 | tf_op jit(solution)/shard_map/psum | solution.py:314
  704.0 189.8 %all-reduce.25.cloned.1.call-done = (f32[640,256]{1,0:T(8,128)}, f32[256,640]{1,0:T(8,128)}, f32[640,512]{1,0:T(8,128)}, f32[640,512]{1,0:T(8,128)}, f32[512,640]{1,0:T(8,128)}) async-done(((f32[640,256]{1,0:T(8,128)}, f32[256,640]{1,0:T(8,128)}, f32[640,512]{1,0:T(8,128)}, f32[640,512]{1,0:T(8,128)}, f32[512,640]{1,0:T(8,128)}), (f32[640,256]{1,0:T(8,128)}, f32[256,640]{1,0:T(8,128)}, ...) | async-done | bytes 5242896 | tf_op jit(solution)/shard_map/psum | solution.py:327
  (296 shorter events, 112.7 us)
Async XLA Ops:
  7.2 188.3 %copy-start = (bf16[512,640]{1,0:T(8,128)(2,1)S(1)}, bf16[512,640]{1,0:T(8,128)(2,1)}, u32[]{:S(2)}) copy-start(bf16[512,640]{1,0:T(8,128)(2,1)} %param.28) | copy-start | bytes 1966084
  7.2 2.6 copy-start.4
  7.2 2.6 copy-start.62
  7.2 173.1 %all-reduce.15.cloned.1.call-start = ((), (), s32[]{:S(2)}) async-start(), calls=%async_computation | async-start | bytes 10485760 | tf_op jit(solution)/shard_map/psum | solution.py:263
  7.3 14.0 %copy-start.66 = (f32[128]{0:T(128)}, f32[128]{0:T(128)S(1)}, u32[]{:S(2)}) copy-start(f32[128]{0:T(128)S(1)} %multiply_power_fusion) | copy-start | bytes 1540
  10.8 4.7 copy-start.15
  13.2 5.4 copy-start.46
  15.5 5.8 copy-start.54
  15.5 3.0 copy-start.68
  15.5 3.0 copy-start.69
  15.5 3.0 copy-start.60
  15.6 5.7 copy-start.44
  18.6 2.7 copy-start.56
  18.6 2.7 copy-start.58
  18.6 2.7 copy-start.48
  35.6 3.7 copy-start.61
  74.9 184.1 %all-reduce.17.cloned.1.call-start = ((), (), s32[]{:S(2)}) async-start(), calls=%async_computation.1 | async-start | bytes 5242880 | tf_op jit(solution)/shard_map/psum | solution.py:266
  180.3 4.0 copy-start.2
  190.1 4.1 copy-start.70
  198.8 139.5 %all-reduce.19.cloned.1.call-start = ((), (), s32[]{:S(2)}) async-start(), calls=%async_computation.2 | async-start | bytes 5242880 | tf_op jit(solution)/shard_map/psum | solution.py:269
  261.5 4.2 copy-start.12
  261.5 5.7 copy-start.73
  267.2 5.6 copy-start.27
  267.9 4.9 copy-start.37
  278.1 288.0 %all-reduce.21.cloned.1.call-start = ((), (), s32[]{:S(2)}) async-start(), calls=%async_computation.3 | async-start | bytes 5242880 | tf_op jit(solution)/shard_map/psum | solution.py:272
  338.3 4.4 copy-start.13
  338.3 4.8 copy-start.18
  342.7 8.2 slice-start
  343.1 7.8 slice-start.1
  484.2 3.7 copy-start.49
  484.2 3.7 copy-start.67
  487.9 7.4 copy-start.8
  487.9 7.4 copy-start.47
  487.9 7.4 copy-start.59
  504.8 199.2 %all-reduce.23.cloned.1.call-start = ((), (), s32[]{:S(2)}) async-start(), calls=%async_computation.4 | async-start | bytes 2621440 | tf_op jit(solution)/shard_map/psum | solution.py:314
  506.5 4.3 copy-start.20
  510.8 2.6 copy-start.16
  510.8 2.6 copy-start.24
  516.9 4.1 copy-start.17
  517.0 376.8 %all-reduce.25.cloned.1.call-start = ((), (), s32[]{:S(2)}) async-start(), calls=%async_computation.5 | async-start | bytes 10485760 | tf_op jit(solution)/shard_map/psum | solution.py:327
  517.0 4.1 copy-start.22
  522.8 43.3 %copy-start.5 = (bf16[2048,640]{1,0:T(8,128)(2,1)S(1)}, bf16[2048,640]{1,0:T(8,128)(2,1)}, u32[]{:S(2)}) copy-start(bf16[2048,640]{1,0:T(8,128)(2,1)} %param.21) | copy-start | bytes 7864324
  563.1 44.7 %copy-start.51 = (f32[2048]{0:T(1024)S(1)}, f32[2048]{0:T(1024)}, u32[]{:S(2)}) copy-start(f32[2048]{0:T(1024)} %copy-done.50) | copy-start | bytes 24580
  704.0 193.9 %copy-start.34 = (f32[640,256]{1,0:T(8,128)S(1)}, f32[640,256]{1,0:T(8,128)}, u32[]{:S(2)}) copy-start(f32[640,256]{1,0:T(8,128)} %get-tuple-element.413) | copy-start | bytes 1966084
  893.8 4.9 copy-start.35
  893.8 5.8 copy-start.33
  897.9 2.7 copy-start.32
  899.6 3.2 copy-start.1
  (34 other events, 55.9 us)
Sparse Core Ops, SparseCore 0:
  75.0 105.2 all-reduce.14
  198.9 60.0 all-reduce.16
  278.3 59.9 all-reduce.18
  504.9 61.2 all-reduce.20
  572.2 131.7 all-reduce.22
  709.3 184.4 all-reduce.24
where the time goes:
time: 920 us; the launch traced here: 910 us
  waiting for transfers between devices  502 us (55%)
  local copies, waits for them, and re-layouts  153 us (17%)
  matrix products  95.9 us (10%)
  blocking collectives  77.9 us (8%)
  other arithmetic  63.7 us (7%)
  between operations  15.2 us (2%)
    psum x1, waiting for transfers between devices, on_device(): lax.psum((grad_query_weight, grad_output_weight, grad_gate_weight, grad_u...  190 us
    psum x1, waiting for transfers between devices, attention_reduce(): return lax.psum(values, 'tensor')  105 us
    dynamic_update_slice x16, local copies, waits for them, and re-layouts, run_layer(): lax.map(attend_back, (query_packs, key_packs, value_packs, segment_packs,...  92.6 us
    psum x1, waiting for transfers between devices, on_device(): lax.psum((grad_key_weight, grad_value_weight, grad_query_norm, grad_key_n...  90.6 us
    psum x1, waiting for transfers between devices, feed_reduce(): return lax.psum(values.astype(jnp.bfloat16), 'tensor').astype(jnp.float32)  59.6 us
    psum x1, waiting for transfers between devices, feed_back_reduce(): return lax.psum(values.astype(jnp.bfloat16), 'tensor').astype(jnp.float32)  54.6 us
    psum x1, blocking collectives, on_device(): lax.psum((grad_key_weight, grad_value_weight, grad_query_norm, grad_key_n...  40.3 us
    psum x1, blocking collectives, on_device(): lax.psum((grad_query_weight, grad_output_weight, grad_gate_weight, grad_u...  37.7 us
  transfers between devices with their start and end apart: 6, of which 6 were waited for; matrix products, arithmetic and copies ran while one was open for 3% of the time, Pallas kernels for 0%

commit v1 on v0

--- a/solution.py
+++ b/solution.py
@@ -260,7 +260,7 @@
 ):
 
     def attention_reduce(values):
-        return lax.psum(values, "tensor")
+        return jnp.sum(lax.all_gather(values, "tensor"), axis=0)
 
     def feed_reduce(values):
         return lax.psum(values.astype(jnp.bfloat16), "tensor").astype(jnp.float32)

time: 920 us -> 961 us (1.045)
  waiting for transfers between devices: 502 us -> 531 us
  other arithmetic: 63.7 us -> 74.4 us
    all_gather x0 -> x1, waiting for transfers between devices: none -> 134 us  [attention_reduce(): return jnp.sum(lax.all_gather(values, 'tensor'), axis=0)]
    psum x1 -> x0, waiting for transfers between devices: 105 us -> none  [attention_reduce(): return lax.psum(values, 'tensor')]
    reduce_sum x0 -> x1, other arithmetic: none -> 10.6 us  [attention_reduce(): return jnp.sum(lax.all_gather(values, 'tensor'), axis=0)]
where the time goes in v1:
time: 961 us; the launch traced here: 950 us
  waiting for transfers between devices  531 us (55%)
  local copies, waits for them, and re-layouts  154 us (16%)
  matrix products  95.8 us (10%)
  blocking collectives  78 us (8%)
  other arithmetic  74.4 us (8%)
  between operations  15.4 us (2%)
    psum x1, waiting for transfers between devices, on_device(): lax.psum((grad_query_weight, grad_output_weight, grad_gate_weight, grad_u...  190 us
    all_gather x1, waiting for transfers between devices, attention_reduce(): return jnp.sum(lax.all_gather(values, 'tensor'), axis=0)  134 us
    dynamic_update_slice x16, local copies, waits for them, and re-layouts, run_layer(): lax.map(attend_back, (query_packs, key_packs, value_packs, segment_packs,...  92.6 us
    psum x1, waiting for transfers between devices, on_device(): lax.psum((grad_key_weight, grad_value_weight, grad_query_norm, grad_key_n...  90.6 us
    psum x1, waiting for transfers between devices, feed_reduce(): return lax.psum(values.astype(jnp.bfloat16), 'tensor').astype(jnp.float32)  59.4 us
    psum x1, waiting for transfers between devices, feed_back_reduce(): return lax.psum(values.astype(jnp.bfloat16), 'tensor').astype(jnp.float32)  54.6 us
    psum x1, blocking collectives, on_device(): lax.psum((grad_key_weight, grad_value_weight, grad_query_norm, grad_key_n...  40.3 us
    psum x1, blocking collectives, on_device(): lax.psum((grad_query_weight, grad_output_weight, grad_gate_weight, grad_u...  37.7 us
  transfers between devices with their start and end apart: 6, of which 6 were waited for; matrix products, arithmetic and copies ran while one was open for 3% of the time, Pallas kernels for 0%

profile of v1, /device:TPU:0, one launch (start us, length us, event | category | flops | bytes accessed | tf_op | source)
XLA Modules:
  0.0 950.1 jit_solution(7494046543512947230)
XLA Ops:
  7.3 2.5 fusion.63
  11.4 2.3 multiply_reduce_fusion.6
  13.7 2.3 multiply_reduce_fusion.5
  16.1 3.0 copy.42
  19.2 2.7 multiply_bitcast_fusion
  21.8 5.7 fusion.99
  31.6 2.3 pad_maximum_fusion
  36.1 3.7 convolution_convert_fusion.4
  40.5 2.3 pad_maximum_fusion.1
  43.8 26.8 %while.26 = (s32[]{:T(128)}, bf16[4,512,1,256]{3,1,0,2:T(8,128)(2,1)}, f32[4,1,512,1]{2,3,1,0:T(1,128)}, bf16[4,512,256]{2,1,0:T(8,128)(2,1)}, s32[4,512]{1,0:T(...) while((s32[]{:T(128)}, bf16[4,512,1,256]{3,1,0,2:T(8,128)(2,1)}, ...), condition=%wide.region_6.7_spmd, body=%wide.region_3.6_spmd.sunk | while | flops 271187456 | bytes 5272153 | solution.py:134
  70.6 4.6 fusion.115
  76.0 133.8 %all-gather.3.cloned.1.call-done = f32[8192,640]{1,0:T(8,128)} async-done(((f32[2048,640]{1,0:T(8,128)}), f32[8192,640]{1,0:T(8,128)}) %all-gather.3.cloned.1.call-update) | async-done | bytes 20971536 | tf_op jit(solution)/shard_map/all_gather | solution.py:263
  209.8 10.6 %reduce_sum.198 = f32[2048,640]{1,0:T(8,128)} reduce(f32[4,2048,640]{2,1,0:T(8,128)} %bitcast.231, f32[]{:T(128)} %constant.85.clone.1), dimensions={0}, to_apply=%region_7.8 | reduce | flops 3932160 | bytes 26214404 | tf_op jit(solution)/shard_map/reduce_sum | solution.py:263
  220.4 3.0 multiply_reduce_fusion.4
  230.1 4.1 multiply_convert_fusion.3
  235.5 3.3 convolution_convert_fusion.2
  239.5 59.4 %all-reduce.14.cloned.1.call-done = bf16[2048,640]{1,0:T(8,128)(2,1)} async-done(((bf16[2048,640]{1,0:T(8,128)(2,1)}), bf16[2048,640]{1,0:T(8,128)(2,1)}) %all-reduce.14.cloned.1.call-update) | async-done | bytes 2621456 | tf_op jit(solution)/shard_map/psum | solution.py:266
  298.9 2.5 fusion.61
  301.4 4.2 fusion.57
  307.8 4.9 multiply_convert_fusion.2
  314.8 3.3 add_convert_fusion.1
  318.5 5.3 fusion.126
  323.7 54.6 %all-reduce.16.cloned.1.call-done = bf16[2048,640]{1,0:T(8,128)(2,1)} async-done(((bf16[2048,640]{1,0:T(8,128)(2,1)}), bf16[2048,640]{1,0:T(8,128)(2,1)}) %all-reduce.16.cloned.1.call-update) | async-done | bytes 2621456 | tf_op jit(solution)/shard_map/psum | solution.py:269
  378.4 4.4 fusion.55
  383.2 7.7 multiply_reduce_fusion.1
  395.9 125.7 %while.27 = (s32[]{:T(128)}, f32[4,512,1,256]{1,0,3,2:T(4,128)}, f32[4,512,1,256]{1,0,3,2:T(4,128)}, bf16[4,512,1,256]{3,1,0,2:T(8,128)(2,1)}, bf16[4,512,256]{2...) while((s32[]{:T(128)}, f32[4,512,1,256]{1,0,3,2:T(4,128)}, ...), condition=%wide.region_18.19_spmd, body=%wide.region_16.18_spmd.sunk | while | flops 674627072 | bytes 16275081 | solution.py:191
  402.1 11.0 %dynamic_update_slice.30 = f32[4,512,1,256]{1,0,3,2:T(4,128)} dynamic-update-slice(f32[4,512,1,256]{1,0,3,2:T(4,128)} %get-tuple-element.385, f32[1,512,1,256]{1,0,3,2:T(1,128)S(1)} %copy.94, s32[]{:T(128)} %get-tuple-element.383, s32[]{:T(128)} %constant.83.clone.1..sunk, s32[]{:T(128)} %constant.83.clone.1..sunk, s32[]{:T(128)} %constant.83.clone.1..sunk) | dynamic-update-slice | bytes 1048580 | tf_op jit(solution)/shard_map/while/body/jit(dynamic_update_index_in_dim)/dynamic_update_slice | solution.py:191
  415.0 11.0 %dynamic_update_slice.29 = f32[4,512,1,256]{1,0,3,2:T(4,128)} dynamic-update-slice(f32[4,512,1,256]{1,0,3,2:T(4,128)} %get-tuple-element.384, f32[1,512,1,256]{1,0,3,2:T(1,128)S(1)} %copy.93, s32[]{:T(128)} %get-tuple-element.383, s32[]{:T(128)} %constant.83.clone.1..sunk, s32[]{:T(128)} %constant.83.clone.1..sunk, s32[]{:T(128)} %constant.83.clone.1..sunk) | dynamic-update-slice | bytes 1048580 | tf_op jit(solution)/shard_map/while/body/jit(dynamic_update_index_in_dim)/dynamic_update_slice | solution.py:191
  433.6 11.0 %dynamic_update_slice.30 = f32[4,512,1,256]{1,0,3,2:T(4,128)} dynamic-update-slice(f32[4,512,1,256]{1,0,3,2:T(4,128)} %get-tuple-element.385, f32[1,512,1,256]{1,0,3,2:T(1,128)S(1)} %copy.94, s32[]{:T(128)} %get-tuple-element.383, s32[]{:T(128)} %constant.83.clone.1..sunk, s32[]{:T(128)} %constant.83.clone.1..sunk, s32[]{:T(128)} %constant.83.clone.1..sunk) | dynamic-update-slice | bytes 1048580 | tf_op jit(solution)/shard_map/while/body/jit(dynamic_update_index_in_dim)/dynamic_update_slice | solution.py:191
  446.4 11.0 %dynamic_update_slice.29 = f32[4,512,1,256]{1,0,3,2:T(4,128)} dynamic-update-slice(f32[4,512,1,256]{1,0,3,2:T(4,128)} %get-tuple-element.384, f32[1,512,1,256]{1,0,3,2:T(1,128)S(1)} %copy.93, s32[]{:T(128)} %get-tuple-element.383, s32[]{:T(128)} %constant.83.clone.1..sunk, s32[]{:T(128)} %constant.83.clone.1..sunk, s32[]{:T(128)} %constant.83.clone.1..sunk) | dynamic-update-slice | bytes 1048580 | tf_op jit(solution)/shard_map/while/body/jit(dynamic_update_index_in_dim)/dynamic_update_slice | solution.py:191
  465.0 11.0 %dynamic_update_slice.30 = f32[4,512,1,256]{1,0,3,2:T(4,128)} dynamic-update-slice(f32[4,512,1,256]{1,0,3,2:T(4,128)} %get-tuple-element.385, f32[1,512,1,256]{1,0,3,2:T(1,128)S(1)} %copy.94, s32[]{:T(128)} %get-tuple-element.383, s32[]{:T(128)} %constant.83.clone.1..sunk, s32[]{:T(128)} %constant.83.clone.1..sunk, s32[]{:T(128)} %constant.83.clone.1..sunk) | dynamic-update-slice | bytes 1048580 | tf_op jit(solution)/shard_map/while/body/jit(dynamic_update_index_in_dim)/dynamic_update_slice | solution.py:191
  477.8 11.0 %dynamic_update_slice.29 = f32[4,512,1,256]{1,0,3,2:T(4,128)} dynamic-update-slice(f32[4,512,1,256]{1,0,3,2:T(4,128)} %get-tuple-element.384, f32[1,512,1,256]{1,0,3,2:T(1,128)S(1)} %copy.93, s32[]{:T(128)} %get-tuple-element.383, s32[]{:T(128)} %constant.83.clone.1..sunk, s32[]{:T(128)} %constant.83.clone.1..sunk, s32[]{:T(128)} %constant.83.clone.1..sunk) | dynamic-update-slice | bytes 1048580 | tf_op jit(solution)/shard_map/while/body/jit(dynamic_update_index_in_dim)/dynamic_update_slice | solution.py:191
  496.4 11.0 %dynamic_update_slice.30 = f32[4,512,1,256]{1,0,3,2:T(4,128)} dynamic-update-slice(f32[4,512,1,256]{1,0,3,2:T(4,128)} %get-tuple-element.385, f32[1,512,1,256]{1,0,3,2:T(1,128)S(1)} %copy.94, s32[]{:T(128)} %get-tuple-element.383, s32[]{:T(128)} %constant.83.clone.1..sunk, s32[]{:T(128)} %constant.83.clone.1..sunk, s32[]{:T(128)} %constant.83.clone.1..sunk) | dynamic-update-slice | bytes 1048580 | tf_op jit(solution)/shard_map/while/body/jit(dynamic_update_index_in_dim)/dynamic_update_slice | solution.py:191
  509.3 11.0 %dynamic_update_slice.29 = f32[4,512,1,256]{1,0,3,2:T(4,128)} dynamic-update-slice(f32[4,512,1,256]{1,0,3,2:T(4,128)} %get-tuple-element.384, f32[1,512,1,256]{1,0,3,2:T(1,128)S(1)} %copy.93, s32[]{:T(128)} %get-tuple-element.383, s32[]{:T(128)} %constant.83.clone.1..sunk, s32[]{:T(128)} %constant.83.clone.1..sunk, s32[]{:T(128)} %constant.83.clone.1..sunk) | dynamic-update-slice | bytes 1048580 | tf_op jit(solution)/shard_map/while/body/jit(dynamic_update_index_in_dim)/dynamic_update_slice | solution.py:191
  521.6 2.7 reshape.588
  524.3 3.7 reshape.591
  528.0 7.4 fusion.104
  542.3 2.5 add_convert_fusion
  546.5 4.3 fusion.124
  550.9 2.6 fusion.125
  557.1 4.1 fusion.123
  562.9 40.3 %all-reduce.4 = (f32[256]{0:T(256)}, f32[256]{0:T(256)}) all-reduce(f32[256]{0:T(256)S(1)} %get-tuple-element.156, f32[256]{0:T(256)S(1)} %get-tuple-element.154), channel_id=1, replica_groups=mesh['dp'=8,'tensor'=4] {'dp','tensor'}, use_global_device_ids=true, to_apply=%region_33.34 | all-reduce | flops 512 | bytes 4096 | tf_op jit(solution)/shard_map/psum | solution.py:314
  603.2 3.0 all-reduce.18.cloned.1.call-done
  606.2 4.0 fusion.56
  610.2 37.7 %all-reduce.6 = (f32[640]{0:T(1024)}, f32[640]{0:T(1024)}, f32[640]{0:T(1024)}, f32[640]{0:T(1024)}) all-reduce(f32[640]{0:T(1024)S(1)} %get-tuple-element.152, f32[640]{0:T(1024)S(1)} %get-tuple-element.146, f32[640]{0:T(1024)S(1)} %get-tuple-element.148, f32[640]{0:T(1024)S(1)} %get-tuple-element.150), channel_id=1, replica_groups=mesh['dp'=8,'tensor'=4] {'dp'}, use_global_device_ids=true, to_apply=%region_31.32 | all-reduce | flops 2560 | bytes 20480 | tf_op jit(solution)/shard_map/psum | solution.py:327
  647.9 5.5 fusion.60
  653.4 90.6 %all-reduce.20.cloned.1.call-done = (f32[640,256]{1,0:T(8,128)}, f32[640,256]{1,0:T(8,128)}) async-done(((f32[640,256]{1,0:T(8,128)}, f32[640,256]{1,0:T(8,128)}), (f32[640,256]{1,0:T(8,128)}, f32[640,256]{1,0:T(8,128)})) %all-reduce.20.cloned.1.call-update) | async-done | bytes 1310736 | tf_op jit(solution)/shard_map/psum | solution.py:314
  744.0 189.8 %all-reduce.22.cloned.1.call-done = (f32[640,256]{1,0:T(8,128)}, f32[256,640]{1,0:T(8,128)}, f32[640,512]{1,0:T(8,128)}, f32[640,512]{1,0:T(8,128)}, f32[512,640]{1,0:T(8,128)}) async-done(((f32[640,256]{1,0:T(8,128)}, f32[256,640]{1,0:T(8,128)}, f32[640,512]{1,0:T(8,128)}, f32[640,512]{1,0:T(8,128)}, f32[512,640]{1,0:T(8,128)}), (f32[640,256]{1,0:T(8,128)}, f32[256,640]{1,0:T(8,128)}, ...) | async-done | bytes 5242896 | tf_op jit(solution)/shard_map/psum | solution.py:327
  (298 shorter events, 115.6 us)
Async XLA Ops:
  7.2 228.3 %copy-start = (bf16[512,640]{1,0:T(8,128)(2,1)S(1)}, bf16[512,640]{1,0:T(8,128)(2,1)}, u32[]{:S(2)}) copy-start(bf16[512,640]{1,0:T(8,128)(2,1)} %param.28) | copy-start | bytes 1966084
  7.2 3.2 copy-start.4
  7.2 3.2 copy-start.62
  7.2 202.6 %all-gather.3.cloned.1.call-start = ((), (), s32[]{:S(2)}) async-start(), calls=%async_computation.3 | async-start | bytes 26214400 | tf_op jit(solution)/shard_map/all_gather | solution.py:263
  7.3 14.5 %copy-start.66 = (f32[128]{0:T(128)}, f32[128]{0:T(128)S(1)}, u32[]{:S(2)}) copy-start(f32[128]{0:T(128)S(1)} %multiply_power_fusion) | copy-start | bytes 1540
  11.4 4.7 copy-start.15
  13.7 5.4 copy-start.46
  16.1 3.0 copy-start.56
  16.1 3.0 copy-start.68
  16.1 3.0 copy-start.69
  16.1 3.0 copy-start.60
  19.1 2.7 copy-start.58
  19.1 2.7 copy-start.48
  36.1 3.7 copy-start.61
  75.3 223.6 %all-reduce.14.cloned.1.call-start = ((), (), s32[]{:S(2)}) async-start(), calls=%async_computation | async-start | bytes 5242880 | tf_op jit(solution)/shard_map/psum | solution.py:266
  220.4 4.0 copy-start.2
  230.1 4.1 copy-start.70
  238.8 139.5 %all-reduce.16.cloned.1.call-start = ((), (), s32[]{:S(2)}) async-start(), calls=%async_computation.1 | async-start | bytes 5242880 | tf_op jit(solution)/shard_map/psum | solution.py:269
  301.4 4.2 copy-start.12
  301.4 5.7 copy-start.73
  307.1 5.6 copy-start.27
  307.8 4.9 copy-start.37
  318.2 288.0 %all-reduce.18.cloned.1.call-start = ((), (), s32[]{:S(2)}) async-start(), calls=%async_computation.2 | async-start | bytes 5242880 | tf_op jit(solution)/shard_map/psum | solution.py:272
  378.4 4.4 copy-start.13
  378.4 4.8 copy-start.18
  382.8 8.2 slice-start
  383.2 7.8 slice-start.1
  524.3 3.7 copy-start.49
  524.3 3.7 copy-start.67
  527.9 7.4 copy-start.8
  528.0 7.4 copy-start.47
  528.0 7.4 copy-start.59
  544.8 199.2 %all-reduce.20.cloned.1.call-start = ((), (), s32[]{:S(2)}) async-start(), calls=%async_computation.4 | async-start | bytes 2621440 | tf_op jit(solution)/shard_map/psum | solution.py:314
  546.5 4.3 copy-start.20
  550.9 2.6 copy-start.16
  550.9 2.6 copy-start.24
  557.0 4.1 copy-start.17
  557.0 376.8 %all-reduce.22.cloned.1.call-start = ((), (), s32[]{:S(2)}) async-start(), calls=%async_computation.5 | async-start | bytes 10485760 | tf_op jit(solution)/shard_map/psum | solution.py:327
  557.0 4.1 copy-start.22
  562.9 43.3 %copy-start.5 = (bf16[2048,640]{1,0:T(8,128)(2,1)S(1)}, bf16[2048,640]{1,0:T(8,128)(2,1)}, u32[]{:S(2)}) copy-start(bf16[2048,640]{1,0:T(8,128)(2,1)} %param.21) | copy-start | bytes 7864324
  562.9 43.3 %copy-start.45 = (f32[2048]{0:T(1024)S(1)}, f32[2048]{0:T(1024)}, u32[]{:S(2)}) copy-start(f32[2048]{0:T(1024)} %copy-done.44) | copy-start | bytes 24580
  562.9 43.3 %copy-start.55 = (f32[640]{0:T(1024)S(1)}, f32[640]{0:T(1024)}, u32[]{:S(2)}) copy-start(f32[640]{0:T(1024)} %copy-done.54) | copy-start | bytes 7684
  603.2 44.7 %copy-start.51 = (f32[2048]{0:T(1024)S(1)}, f32[2048]{0:T(1024)}, u32[]{:S(2)}) copy-start(f32[2048]{0:T(1024)} %copy-done.50) | copy-start | bytes 24580
  744.0 193.9 %copy-start.34 = (f32[640,256]{1,0:T(8,128)S(1)}, f32[640,256]{1,0:T(8,128)}, u32[]{:S(2)}) copy-start(f32[640,256]{1,0:T(8,128)} %get-tuple-element.411) | copy-start | bytes 1966084
  933.8 4.9 copy-start.35
  933.8 5.8 copy-start.33
  937.9 2.7 copy-start.32
  939.6 3.2 copy-start.1
  (34 other events, 53.4 us)
Sparse Core Ops, SparseCore 0:
  75.4 134.3 all-gather.2
  238.9 59.8 all-reduce.13
  318.3 60.0 all-reduce.15
  545.0 61.2 all-reduce.17
  612.2 131.7 all-reduce.19
  749.3 184.4 all-reduce.21
